TPU v7x, 32 devices: a whole 2x2x4 slice. The times are simulated.
32 devices in a mesh: groups: 2 (over y), pts: 4 (over z), freq: 2 (over x), sub: 2 (over core).
Axes of the slice: x: 2, y: 2, z: 4, core: 2. Of those that a mesh axis runs over, the one named last changes fastest.
Arguments:
- series: bfloat16 [2048, 8, 16384], P(('pts', 'sub'), 'freq', 'groups'), parts along dimension 2, may hold values from -256 to 256, as said below
- block_start: int32 [15], replicated, may hold values from 0 to 1792, as said below
- freq_index: int32 [64], replicated, may hold values from 0 to 128, as said below
Outputs:
- modes: float32 [2, 64, 16, 8192], P(None, 'freq', 'groups', ('pts', 'sub')), parts along dimension 2
- spectrum: float32 [128], P(('groups', 'freq')), parts along dimension 0
There are 2 independent parts, one for each index of `groups`. A program takes and returns all parts, laid end to end along the dimension named above; an argument that names none is the same for every part. Nothing has to cross between parts.
Inputs may be any that keep to these rules, and one draw needn't show every extreme that they name: series is finite. block_start rises with the block; its first entry is 0 and its last is 1792; every other entry lies within 32 of its block number times 128. freq_index holds 64 different bins, 0 and 128 among them.
All inputs are finite; a program needn't handle non-finite values.
Results may differ from a plain program's by a relative error of at most 0.0041.
Values may be sent and summed in bfloat16 or wider, within the bound.
A program may use at most 128 MiB of HBM per device.

v0:
```python
import math

import jax
import jax.numpy as jnp
from jax import lax
from jax.sharding import PartitionSpec as P

NFFT = 256
ITERS = 3


def dft_basis(freq_index, window_len):
    steps_int = jnp.arange(window_len, dtype=jnp.int32)
    phase_int = freq_index[:, None] * steps_int[None, :] % window_len
    angle = 2.0 * math.pi / window_len * phase_int.astype(jnp.float32)
    window = 0.5 - 0.5 * jnp.cos(2.0 * math.pi / window_len * steps_int.astype(jnp.float32))
    weighting = window / jnp.sqrt(jnp.sum(window * window))
    table = jnp.stack([jnp.cos(angle), -jnp.sin(angle)], axis=1) * weighting[None, None, :]
    return table.reshape(-1, window_len).astype(jnp.bfloat16)


def apply_cross(cross_real, cross_imag, vec_real, vec_imag):
    highest = lax.Precision.HIGHEST
    out_real = jnp.einsum("kbd,kd->kb", cross_real, vec_real, precision=highest) - jnp.einsum(
        "kbd,kd->kb", cross_imag, vec_imag, precision=highest
    )
    out_imag = jnp.einsum("kbd,kd->kb", cross_real, vec_imag, precision=highest) + jnp.einsum(
        "kbd,kd->kb", cross_imag, vec_real, precision=highest
    )
    return (out_real, out_imag)


def leading_vector(cross_real, cross_imag, sweeps):
    initial = jnp.full(cross_real.shape[:2], 1.0 / math.sqrt(cross_real.shape[1]), jnp.float32)
    vec_real = initial
    vec_imag = jnp.zeros_like(initial)
    for sweep_index in range(sweeps):
        out_real, out_imag = apply_cross(cross_real, cross_imag, vec_real, vec_imag)
        length = jnp.sqrt(jnp.sum(out_real * out_real + out_imag * out_imag, axis=1, keepdims=True))
        vec_real = out_real / length
        vec_imag = out_imag / length
    out_real, out_imag = apply_cross(cross_real, cross_imag, vec_real, vec_imag)
    spectrum = jnp.sum(vec_real * out_real + vec_imag * out_imag, axis=1)
    return (vec_real, vec_imag, spectrum)


def cross_spectra(coefficients):
    product = jnp.einsum(
        "bkcxr,dkexr->kcebd", coefficients, coefficients, preferred_element_type=jnp.float32
    )
    return (product[:, 0, 0] + product[:, 1, 1], product[:, 0, 1] - product[:, 1, 0])


def project_modes(coefficients, vec_real, vec_imag):
    low_real = vec_real.astype(jnp.bfloat16)
    low_imag = vec_imag.astype(jnp.bfloat16)
    mixing = jnp.stack(
        [jnp.stack([low_real, low_imag], axis=1), jnp.stack([-low_imag, low_real], axis=1)], axis=1
    )
    raw_modes = jnp.einsum(
        "bkcxr,kceb->ekxr", coefficients, mixing, preferred_element_type=jnp.float32
    )
    return (low_real, low_imag, raw_modes)


def shards(series, block_start, freq_index):
    snap_rows, slab_rows, plane = series.shape
    group_count = lax.axis_size(("pts", "sub"))
    width = plane // group_count
    tiles_in = series.reshape(1, snap_rows, slab_rows, group_count, width)
    regrouped = lax.all_to_all(tiles_in, ("pts", "sub"), split_axis=3, concat_axis=0, tiled=True)
    history = regrouped.reshape(-1, slab_rows * width)
    basis = dft_basis(freq_index, NFFT)

    def one_block(carried, offset):
        segment = lax.dynamic_slice_in_dim(history, offset, NFFT, 0)
        return (
            carried,
            jnp.dot(basis, segment, preferred_element_type=jnp.float32).astype(jnp.bfloat16),
        )

    unused, tiles = lax.scan(one_block, jnp.int32(0), block_start)
    blocks = block_start.shape[0]
    retained = freq_index.shape[0]
    coefficients = tiles.reshape(blocks, retained, 2, slab_rows, width)
    total_points = slab_rows * lax.axis_size("freq") * plane
    norm_scale = 1.0 / (blocks * total_points)
    moved = lax.all_to_all(coefficients, "freq", split_axis=1, concat_axis=3, tiled=True)
    cross_real, cross_imag = cross_spectra(moved)
    cross_real, cross_imag = lax.psum((cross_real, cross_imag), ("pts", "sub"))
    cross_real = cross_real * norm_scale
    cross_imag = cross_imag * norm_scale
    vec_real, vec_imag, spectrum = leading_vector(cross_real, cross_imag, ITERS)
    low_real, low_imag, raw_modes = project_modes(moved, vec_real, vec_imag)
    partial_energy = jnp.sum(raw_modes[0] * raw_modes[0] + raw_modes[1] * raw_modes[1], axis=(1, 2))
    energy = lax.psum(partial_energy, ("pts", "sub")) / total_points
    modes = raw_modes * lax.rsqrt(energy + 1e-06)[None, :, None, None]
    return (modes, spectrum)


def solution(mesh):
    in_specs = (P(("pts", "sub"), "freq", "groups"), P(), P())
    out_specs = (P(None, "freq", "groups", ("pts", "sub")), P(("groups", "freq")))
    return jax.shard_map(shards, mesh=mesh, in_specs=in_specs, out_specs=out_specs, check_vma=False)
```

profile of v0, /device:TPU:0, one launch (start us, length us, event | category | flops | bytes accessed | tf_op | source)
XLA Modules:
  0.0 892.3 jit_solution(4202417993309503555)
XLA Ops:
  0.6 26.1 %copy.95 = bf16[256,4,8192]{0,2,1:T(8,128)(2,1)} copy(bf16[256,4,8192]{2,1,0:T(4,128)(2,1)} %param.5) | data formatting | bytes 33554432 | tf_op args[0]
  26.8 28.1 %copy.96 = bf16[1,256,4,8,1024]{4,2,1,0,3:T(4,128)(2,1)} copy(bf16[1,256,4,8,1024]{1,4,3,2,0:T(8,128)(2,1)} %bitcast.127) | data formatting | bytes 33554432 | tf_op jit(solution)/shard_map/reshape | solution.py:70
  54.8 6.5 all-to-all-start
  63.3 361.8 %all-to-all-done = bf16[1,256,4,8,1024]{4,2,1,0,3:T(4,128)(2,1)} async-done(((bf16[1,256,4,8,1024]{4,2,1,0,3:T(4,128)(2,1)}), bf16[1,256,4,8,1024]{4,2,1,0,3:T(4,128)(2,1)}, u32[]{:S(2)}, u32[]{:S(2)}) %all-to-all-start) | async-done | bytes 16777248 | tf_op jit(solution)/shard_map/all_to_all | solution.py:71
  425.1 17.0 %copy.198 = bf16[256,8,4,1024]{3,1,2,0:T(8,128)(2,1)} copy(bf16[256,8,4,1024]{3,2,1,0:T(4,128)(2,1)} %bitcast.56) | data formatting | bytes 33554432
  442.2 97.7 %while.10 = (s32[]{:T(128)}, bf16[15,128,4096]{2,1,0:T(8,128)(2,1)}, s32[15]{0:T(128)S(1)}, bf16[2048,4096]{1,0:T(8,128)(2,1)}, bf16[128,256]{1,0:T(8,128)(2,1)S(1)}, /*index=5*/s32[]{:T(128)}, s32[]{:T(128)}, s32[]{:T(128)}) while((s32[]{:T(128)}, bf16[15,128,4096]{2,1,0:T(8,128)(2,1)}, s32[15]{0:T(128)S(1)}, bf16[2048,4096]{1,0:T(8,128)(2,1)}, ...), condition=%wide.region_2.3_spmd, body=%wide.region_1.2_spmd.sunk | while | flops 268959744 | bytes 7406215 | solution.py:82
  444.7 2.4 fusion.52
  470.8 2.4 fusion.52
  477.3 2.4 fusion.52
  483.7 2.4 fusion.52
  490.3 2.4 fusion.52
  503.3 2.4 fusion.52
  509.8 2.4 fusion.52
  516.4 2.4 fusion.52
  529.4 2.4 fusion.52
  539.9 26.2 %reshape.139 = bf16[15,64,2,4,1024]{4,3,2,1,0:T(4,128)(2,1)} reshape(bf16[15,128,4096]{2,1,0:T(8,128)(2,1)} %get-tuple-element.29) | data formatting | bytes 31457280 | tf_op jit(solution)/shard_map/reshape | solution.py:85
  566.1 8.3 copy.99
  574.4 175.4 %all_to_all.33 = bf16[15,64,2,4,1024]{4,3,2,0,1:T(4,128)(2,1)S(1)} all-to-all(bf16[15,64,2,4,1024]{4,3,2,0,1:T(4,128)(2,1)S(1)} %copy.99), channel_id=1, replica_groups=mesh['groups'=2,'pts'=4,'freq'=2,'sub'=2] {'freq'}, dimensions={1} | all-to-all | bytes 31457280 | tf_op jit(solution)/shard_map/all_to_all | solution.py:88
  749.8 21.2 %copy.100 = bf16[15,64,2,4,1024]{4,1,3,2,0:T(8,128)(2,1)S(1)} copy(bf16[15,64,2,4,1024]{4,3,2,0,1:T(4,128)(2,1)S(1)} %all_to_all.33) | data formatting | bytes 31457280 | tf_op jit(solution)/shard_map/all_to_all | solution.py:88
  771.0 20.8 %copy.101 = bf16[15,32,2,2,4,1024]{5,0,4,3,2,1:T(8,128)(2,1)} copy(bf16[15,32,2,2,4,1024]{5,1,3,4,2,0:T(8,128)(2,1)S(1)} %bitcast.128) | data formatting | bytes 31457280 | tf_op jit(solution)/shard_map/all_to_all | solution.py:88
  791.8 34.2 %convolution_bitcast_fusion = f32[32,2,2,15,15]{3,4,1,2,0:T(8,128)S(1)} fusion(bf16[15,32,2,8,1024,1]{4,0,3,5,2,1:T(8,128)(2,1)} %bitcast.130, bf16[15,32,2,8,1024,1]{4,0,3,2,5,1:T(8,128)(2,1)} %bitcast.131), kind=kOutput, calls=%fused_computation.8 | convolution fusion | flops 471859200 | bytes 31572480 | tf_op jit(solution)/shard_map/bkcxr,dkexr->kcebd/dot_general | solution.py:48
  826.1 33.5 %all-reduce = (f32[32,15,15]{1,2,0:T(8,128)S(1)}, f32[32,15,15]{1,2,0:T(8,128)S(1)}) all-reduce(f32[32,15,15]{1,2,0:T(8,128)S(1)} %fusion.12, f32[32,15,15]{1,2,0:T(8,128)S(1)} %fusion.10), channel_id=1, replica_groups=mesh['groups'=2,'pts'=4,'freq'=2,'sub'=2] {'pts','sub'}, use_global_device_ids=true, to_apply=%region_3.4 | all-reduce | flops 14400 | bytes 115200 | tf_op jit(solution)/shard_map/psum | solution.py:90
  864.6 8.1 fusion.5
  874.9 13.6 %psum.23 = f32[32]{0:T(128)S(1)} all-reduce(f32[32]{0:T(128)S(1)} %fusion.9), channel_id=1, replica_groups=mesh['groups'=2,'pts'=4,'freq'=2,'sub'=2] {'pts','sub'}, use_global_device_ids=true, to_apply=%region_9.10 | all-reduce | flops 32 | bytes 256 | tf_op jit(solution)/shard_map/psum | solution.py:96
  (117 shorter events, 59.0 us)
Async XLA Ops:
  54.8 6.5 copy-start
  54.8 370.3 %all-to-all-start = ((bf16[1,256,4,8,1024]{4,2,1,0,3:T(4,128)(2,1)}), bf16[1,256,4,8,1024]{4,2,1,0,3:T(4,128)(2,1)}, u32[]{:S(2)}, u32[]{:S(2)}) async-start(bf16[1,256,4,8,1024]{4,2,1,0,3:T(4,128)(2,1)} %copy.96), calls=%async_computation | async-start | bytes 33554432 | tf_op jit(solution)/shard_map/all_to_all | solution.py:71
  425.1 17.0 %copy-start.1 = (s32[15]{0:T(128)S(1)}, s32[15]{0:T(128)}, u32[]{:S(2)}) copy-start(s32[15]{0:T(128)} %param.6) | copy-start | bytes 184
where the time goes:
time: 896 us; the launch traced here: 892 us
  waiting for transfers between devices  362 us (40%)
  blocking collectives  223 us (25%)
  local copies, waits for them, and re-layouts  184 us (21%)
  matrix products  79.6 us (9%)
  loops' own time  29.4 us (3%)
    all_to_all x1, waiting for transfers between devices, shards(): lax.all_to_all(tiles_in, ('pts', 'sub'), split_axis=3, concat_axis=0, til...  362 us
    all_to_all x1, blocking collectives, shards(): lax.all_to_all(coefficients, 'freq', split_axis=1, concat_axis=3, tiled=T...  175 us
    unnamed x13, local copies, waits for them, and re-layouts  45.6 us
    all_to_all x2, local copies, waits for them, and re-layouts, shards(): lax.all_to_all(coefficients, 'freq', split_axis=1, concat_axis=3, tiled=T...  42 us
    dot_general x15, matrix products, one_block(): jnp.dot(basis, segment, preferred_element_type=jnp.float32)  35.7 us
    reshape x2, local copies, waits for them, and re-layouts, shards(): coefficients = tiles.reshape(blocks, retained, 2, slab_rows, width)  34.5 us
    dot_general x1, matrix products, cross_spectra(): jnp.einsum('bkcxr,dkexr->kcebd', coefficients, coefficients, preferred_el...  34.2 us
    psum x1, blocking collectives, shards(): cross_real, cross_imag = lax.psum((cross_real, cross_imag), ('pts', 'sub'))  33.5 us
  transfers between devices with their start and end apart: 1, of which 1 were waited for; matrix products, arithmetic and copies ran while one was open for 0% of the time, Pallas kernels for 0%

commit v1 on v0

v1 whole, which is shorter than its diff:
```python
import functools
import math

import jax
import jax.numpy as jnp
from jax import lax
from jax.experimental import pallas as pl
from jax.experimental.pallas import tpu as pltpu
from jax.sharding import PartitionSpec as P

NFFT = 256
ITERS = 3
SPACING = 128
JITTER = 32
SPAN = NFFT + 2 * JITTER
PACK = 8
AHEAD = 3
MESH = pl.DeviceIdType.MESH
F32 = jnp.float32
BF16 = jnp.bfloat16
HIGHEST = lax.Precision.HIGHEST


def dft_basis(freq_index, window_len):
    steps_int = jnp.arange(window_len, dtype=jnp.int32)
    phase_int = freq_index[:, None] * steps_int[None, :] % window_len
    angle = 2.0 * math.pi / window_len * phase_int.astype(F32)
    window = 0.5 - 0.5 * jnp.cos(2.0 * math.pi / window_len * steps_int.astype(F32))
    weighting = window / jnp.sqrt(jnp.sum(window * window))
    table = jnp.stack([jnp.cos(angle), -jnp.sin(angle)], axis=1) * weighting[None, None, :]
    return table.reshape(-1, window_len).astype(BF16)


def iota(shape, dim):
    return lax.broadcasted_iota(jnp.int32, shape, dim)


def exact_dot(a, b):
    return lax.dot_general(a, b, (((1,), (0,)), ((), ())), precision=HIGHEST, preferred_element_type=F32)


def kernel(
    cfg, start_ref, basis_ref, series_ref, modes_ref, spec_ref,
    hist, coef, moved, shifted, gram, packed, parts, total,
    own_sem, z_send, z_recv, x_send, x_recv, s_send, s_recv, g_send, g_recv,
):
    npts, nsub, nfreq, snaps, planes, width, cols, blocks, groups, share = cfg
    n = npts * nsub
    pieces = width // cols
    chunks = planes * pieces
    local = groups // nfreq
    rows = blocks * 2 * PACK
    length = n * snaps
    points = planes * nfreq * n * width
    me = lax.axis_index("pts") * nsub + lax.axis_index("sub")
    mine = lax.axis_index("freq")

    def z_device(i):
        other = lax.rem(me + i, n)
        return other, {"pts": other // nsub, "sub": lax.rem(other, nsub)}

    def x_device(i):
        other = lax.rem(mine + i, nfreq)
        return other, {"freq": other}

    barrier = pltpu.get_barrier_semaphore()

    @pl.loop(1, n)
    def _(i):
        pl.semaphore_signal(barrier, inc=1, device_id=z_device(i)[1], device_id_type=MESH)

    @pl.loop(1, nfreq)
    def _(i):
        pl.semaphore_signal(barrier, inc=1, device_id=x_device(i)[1], device_id_type=MESH)

    pl.semaphore_wait(barrier, n - 1 + nfreq - 1)

    def z_copy(c, i):
        other, where = z_device(i)
        at = pl.multiple_of(other * width + lax.rem(c, pieces) * cols, cols)
        return pltpu.make_async_remote_copy(
            src_ref=series_ref.at[c // pieces, :, pl.ds(at, cols)],
            dst_ref=hist.at[c, pl.ds(pl.multiple_of(me * snaps, snaps), snaps)],
            send_sem=z_send.at[c, i],
            recv_sem=z_recv.at[c, i],
            device_id=where,
            device_id_type=MESH,
        )

    def own_copy(c):
        at = pl.multiple_of(me * width + lax.rem(c, pieces) * cols, cols)
        return pltpu.make_async_copy(
            series_ref.at[c // pieces, :, pl.ds(at, cols)],
            hist.at[c, pl.ds(pl.multiple_of(me * snaps, snaps), snaps)],
            own_sem.at[c],
        )

    def x_copy(c, i):
        other, where = x_device(i)
        return pltpu.make_async_remote_copy(
            src_ref=coef.at[c, pl.ds(other * local, local)],
            dst_ref=moved.at[i - 1, c],
            send_sem=x_send.at[c, i],
            recv_sem=x_recv.at[c, i],
            device_id=where,
            device_id_type=MESH,
        )

    def z_start(c):
        @pl.loop(1, n)
        def _(i):
            z_copy(c, i).start()

        own_copy(c).start()

    ahead = min(AHEAD, chunks)
    for c in range(ahead):
        z_start(c)

    firsts = [min(max(SPACING * b - JITTER, 0), length - SPAN) for b in range(blocks)]
    gap = iota((NFFT, SPAN), 1) - iota((NFFT, SPAN), 0)
    for b in range(blocks):
        move = jnp.where(gap == start_ref[b] - firsts[b], 1.0, 0.0).astype(BF16)
        shifted[b] = jnp.dot(basis_ref[...], move, preferred_element_type=F32).astype(BF16)
    gram[...] = jnp.zeros_like(gram)

    def add_gram(g, tile):
        gram[g] += lax.dot_general(tile, tile, (((1,), (1,)), ((), ())), preferred_element_type=F32)

    def take_moved(c):
        @pl.loop(1, nfreq)
        def _(i):
            x_copy(c, i).wait_recv()
            for g in range(local):
                add_gram(g, moved[i - 1, c, g])

    @pl.loop(0, chunks)
    def _(c):
        @pl.when(c + ahead < chunks)
        def _():
            z_start(c + ahead)

        own_copy(c).wait()

        @pl.loop(1, n)
        def _(i):
            z_copy(c, i).wait_recv()

        for b in range(blocks):
            out = jnp.dot(shifted[b], hist[c, firsts[b] : firsts[b] + SPAN, :], preferred_element_type=F32)
            coef[c, :, b * 2 * PACK : (b + 1) * 2 * PACK, :] = out.astype(BF16).reshape(groups, 2 * PACK, cols)

        @pl.loop(1, nfreq)
        def _(i):
            x_copy(c, i).start()

        for g in range(local):
            add_gram(g, coef[c, mine * local + g])

        @pl.when(c > 0)
        def _():
            take_moved(c - 1)

    take_moved(chunks - 1)

    row, col = iota((rows, rows), 0), iota((rows, rows), 1)
    same = jnp.where((row // 2) % PACK == (col // 2) % PACK, 1.0, 0.0).astype(F32)
    eye = row == col
    turn = jnp.where(
        (row // 2 == col // 2) & (row != col), jnp.where(row % 2 == 0, -1.0, 1.0), 0.0
    ).astype(F32)
    lanes = packed.shape[1]
    slot_r, slot_l = iota((rows, lanes), 0), iota((rows, lanes), 1)
    place = slot_r // (2 * PACK) * 2 + slot_r % 2
    slots = 32

    def chooser(g):
        return jnp.where(slot_l == g * slots + place, 1.0, 0.0).astype(F32)

    packed[...] = jnp.zeros_like(packed)
    for g in range(local):
        packed[:rows, :] += exact_dot(gram[g] * same, chooser(g))

    def s_copy(i):
        other, where = z_device(i)
        return pltpu.make_async_remote_copy(
            src_ref=packed.at[pl.ds(pl.multiple_of(other * share, share), share)],
            dst_ref=parts.at[me],
            send_sem=s_send.at[i],
            recv_sem=s_recv.at[i],
            device_id=where,
            device_id_type=MESH,
        )

    def g_copy(i):
        here = pl.ds(pl.multiple_of(me * share, share), share)
        return pltpu.make_async_remote_copy(
            src_ref=total.at[here],
            dst_ref=total.at[here],
            send_sem=g_send.at[i],
            recv_sem=g_recv.at[i],
            device_id=z_device(i)[1],
            device_id_type=MESH,
        )

    here = pl.ds(pl.multiple_of(me * share, share), share)

    @pl.loop(1, n)
    def _(i):
        s_copy(i).start()

    parts[me] = packed[here, :]

    @pl.loop(1, n)
    def _(i):
        s_copy(i).wait()

    total[here, :] = jnp.sum(parts[...], axis=0)

    @pl.loop(1, n)
    def _(i):
        g_copy(i).start()

    @pl.loop(1, n)
    def _(i):
        g_copy(i).wait()

    scale = 1.0 / (blocks * points)
    head = jnp.where(iota((1, rows), 1) % 2 == 0, 1.0 / math.sqrt(blocks), 0.0).astype(F32)
    mode_r, mode_c = iota((2 * PACK, rows), 0), iota((2 * PACK, rows), 1)
    mode_same = mode_r % PACK == (mode_c // 2) % PACK
    mode_first = mode_c == (mode_r % PACK) * 2

    def over(mat, vec):
        return jnp.sum(mat * vec, axis=1, keepdims=True)

    def down(mat, vec):
        return jnp.sum(mat * vec, axis=0, keepdims=True)

    def upright(vec):
        return jnp.sum(jnp.where(eye, vec, 0.0), axis=1, keepdims=True)

    def flat(vec):
        return jnp.sum(jnp.where(eye, vec, 0.0), axis=0, keepdims=True)

    mixes, gains = [], []
    for g in range(local):
        choose = chooser(g)
        block = lax.dot_general(
            total[:rows, :], choose, (((1,), (1,)), ((), ())), precision=HIGHEST, preferred_element_type=F32
        ) * same
        both = (block - exact_dot(exact_dot(turn, block), turn)) * scale
        vec = head
        for _ in range(ITERS):
            out = over(both, vec)
            vec = flat(out) / jnp.sqrt(down(same, out * out))
        spec_ref[g : g + 1, :] = down(same, over(both, vec) * upright(vec))
        low_bf = vec.astype(BF16)
        low = low_bf.astype(F32)
        low_up = upright(low)
        energy = down(same, over(both, low) * low_up) * (points * blocks / points)
        gain = lax.rsqrt(energy + 1e-06)
        turned = flat(over(turn, low))
        mix = jnp.where(mode_same, jnp.where(mode_r < PACK, low, turned), 0.0)
        mixes.append(mix.astype(BF16))
        gains.append(jnp.sum(jnp.where(mode_first, gain, 0.0), axis=1, keepdims=True))

    @pl.loop(0, planes)
    def _(p):
        for q in range(pieces):
            c = p * pieces + q
            at = pl.ds(q * cols, cols)
            for g in range(local):
                modes_ref[mine * planes + p, pl.ds(g * 2 * PACK, 2 * PACK), at] = (
                    jnp.dot(mixes[g], coef[c, mine * local + g], preferred_element_type=F32) * gains[g]
                )
            for i in range(1, nfreq):
                source = lax.rem(mine + nfreq - i, nfreq)
                for g in range(local):
                    modes_ref[source * planes + p, pl.ds(g * 2 * PACK, 2 * PACK), at] = (
                        jnp.dot(mixes[g], moved[i - 1, c, g], preferred_element_type=F32) * gains[g]
                    )

    @pl.loop(0, chunks)
    def _(c):
        @pl.loop(1, n)
        def _(i):
            z_copy(c, i).wait_send()

        @pl.loop(1, nfreq)
        def _(i):
            x_copy(c, i).wait_send()


def shards(series, block_start, freq_index):
    snaps, planes, plane = series.shape
    npts, nsub, nfreq = (lax.axis_size(a) for a in ("pts", "sub", "freq"))
    n = npts * nsub
    width = plane // n
    cols = min(256, width)
    blocks = block_start.shape[0]
    retained = freq_index.shape[0]
    groups = retained // PACK
    local = groups // nfreq
    rows = blocks * 2 * PACK
    chunks = planes * (width // cols)
    share = -(-rows // (8 * n)) * 8
    lanes = max(128, local * 32)
    basis = dft_basis(freq_index, NFFT)
    turned = jnp.transpose(series, (1, 0, 2))
    cfg = (npts, nsub, nfreq, snaps, planes, width, cols, blocks, groups, share)
    dma = pltpu.SemaphoreType.DMA
    raw, spec = pl.pallas_call(
        functools.partial(kernel, cfg),
        out_shape=(
            jax.ShapeDtypeStruct((nfreq * planes, local * 2 * PACK, width), F32),
            jax.ShapeDtypeStruct((local, rows), F32),
        ),
        in_specs=[
            pl.BlockSpec(memory_space=pltpu.SMEM),
            pl.BlockSpec(memory_space=pltpu.VMEM),
            pl.BlockSpec(memory_space=pl.ANY),
        ],
        out_specs=(pl.BlockSpec(memory_space=pltpu.VMEM), pl.BlockSpec(memory_space=pltpu.VMEM)),
        scratch_shapes=[
            pltpu.VMEM((chunks, n * snaps, cols), BF16),
            pltpu.VMEM((chunks, groups, rows, cols), BF16),
            pltpu.VMEM((nfreq - 1, chunks, local, rows, cols), BF16),
            pltpu.VMEM((blocks, 2 * retained, SPAN), BF16),
            pltpu.VMEM((local, rows, rows), F32),
            pltpu.VMEM((n * share, lanes), F32),
            pltpu.VMEM((n, share, lanes), F32),
            pltpu.VMEM((n * share, lanes), F32),
            dma((chunks,)),
            dma((chunks, n)),
            dma((chunks, n)),
            dma((chunks, nfreq)),
            dma((chunks, nfreq)),
            dma((n,)),
            dma((n,)),
            dma((n,)),
            dma((n,)),
        ],
        compiler_params=pltpu.CompilerParams(
            collective_id=0, has_side_effects=True, vmem_limit_bytes=60 * 1024 * 1024
        ),
    )(block_start, basis, turned)
    modes = raw.reshape(nfreq * planes, local, 2, PACK, width).transpose(2, 1, 3, 0, 4)
    modes = modes.reshape(2, local * PACK, nfreq * planes, width)
    return modes, spec[:, : 2 * PACK : 2].reshape(local * PACK)


def solution(mesh):
    in_specs = (P(("pts", "sub"), "freq", "groups"), P(), P())
    out_specs = (P(None, "freq", "groups", ("pts", "sub")), P(("groups", "freq")))
    return jax.shard_map(shards, mesh=mesh, in_specs=in_specs, out_specs=out_specs, check_vma=False)
```

time: 896 us -> 432 us (0.48)
  Pallas kernels: 0 us -> 404 us
  waiting for transfers between devices: 362 us -> 0 us
  blocking collectives: 223 us -> 0 us
  local copies, waits for them, and re-layouts: 184 us -> 24.2 us
  matrix products: 79.6 us -> 0 us
  loops' own time: 29.4 us -> 0 us
    pallas_call x0 -> x1, Pallas kernels: none -> 404 us  [shards(): pl.pallas_call(functools.partial(kernel, cfg), out_shape=(jax.ShapeDtypeS...]
    all_to_all x1 -> x0, waiting for transfers between devices: 362 us -> none  [shards(): lax.all_to_all(tiles_in, ('pts', 'sub'), split_axis=3, concat_axis=0, til...]
    all_to_all x1 -> x0, blocking collectives: 175 us -> none  [shards(): lax.all_to_all(coefficients, 'freq', split_axis=1, concat_axis=3, tiled=T...]
    dot_general x21 -> x0, matrix products: 79.6 us -> none  [the longest x15 35.7 us: one_block(): jnp.dot(basis, segment, preferred_element_type=jnp.float32)]
    reshape x3 -> x1, local copies, waits for them, and re-layouts: 62.6 us -> 0.6 us  [shards(): return (modes, spec[:, :2 * PACK:2].reshape(local * PACK))]
    psum x2 -> x0, blocking collectives: 47.1 us -> none  [the longest x1 33.5 us: shards(): cross_real, cross_imag = lax.psum((cross_real, cross_imag), ('pts', 'sub'))]
    all_to_all x2 -> x0, local copies, waits for them, and re-layouts: 42 us -> none  [shards(): lax.all_to_all(coefficients, 'freq', split_axis=1, concat_axis=3, tiled=T...]
    another operation x1 -> x0, loops' own time: 29.4 us -> none  [shards(): unused, tiles = lax.scan(one_block, jnp.int32(0), block_start)]
  transfers between devices with their start and end apart: 1 -> 0, of which waited for: 1 -> 0; matrix products, arithmetic and copies ran while one was open for 0% -> 0% of each run, Pallas kernels for 0% -> 0%
where the time goes in v1:
time: 432 us
  Pallas kernels  404 us (94%)
  local copies, waits for them, and re-layouts  24.2 us (6%)
    pallas_call x1, Pallas kernels, shards(): pl.pallas_call(functools.partial(kernel, cfg), out_shape=(jax.ShapeDtypeS...  404 us
    unnamed x1, local copies, waits for them, and re-layouts  18.5 us

profile of v1, /device:TPU:0, one launch (start us, length us, event | category | flops | bytes accessed | tf_op | source)
XLA Modules:
  0.0 431.9 jit_solution(5520909120750648428)
XLA Ops:
  0.6 0.6 multiply_reduce_fusion
  2.0 1.0 fusion.6
  3.0 0.1 copy.7
  3.1 0.1 stack.8
  3.2 0.6 multiply_convert_fusion.basis_ref
  3.9 18.5 %copy.11 = bf16[256,4,8192]{2,0,1:T(8,128)(2,1)} copy(bf16[256,4,8192]{2,1,0:T(4,128)(2,1)} %param.3) | data formatting | bytes 33554432 | tf_op args[0]
  22.4 404.0 %shard_map.50 = (f32[8,64,1024]{2,1,0:T(8,128)}, f32[4,240]{1,0:T(4,128)}) custom-call(s32[15]{0:T(128)} %start_ref.1, bf16[128,256]{1,0:T(8,128)(2,1)} %multiply_convert_fusion.basis_ref, bf16[4,256,8192]{2,1,0:T(8,128)(2,1)} %bitcast.7), custom_call_target="tpu_custom_call" | custom-call | tf_op jit(solution)/shard_map/pallas_call | solution.py:313
  426.4 4.2 copy.9
  430.5 0.8 slice.3
  431.3 0.6 reshape.120
  (2 shorter events, 0.1 us)

commit v2 on v1

--- a/solution.py
+++ b/solution.py
@@ -14,21 +14,23 @@
 JITTER = 32
 SPAN = NFFT + 2 * JITTER
 PACK = 8
-AHEAD = 3
 MESH = pl.DeviceIdType.MESH
 F32 = jnp.float32
 BF16 = jnp.bfloat16
 HIGHEST = lax.Precision.HIGHEST
 
 
-def dft_basis(freq_index, window_len):
-    steps_int = jnp.arange(window_len, dtype=jnp.int32)
-    phase_int = freq_index[:, None] * steps_int[None, :] % window_len
-    angle = 2.0 * math.pi / window_len * phase_int.astype(F32)
-    window = 0.5 - 0.5 * jnp.cos(2.0 * math.pi / window_len * steps_int.astype(F32))
+def dft_basis(freq_ref, retained):
+    shape = (2 * retained, NFFT)
+    row, step = iota(shape, 0), iota(shape, 1)
+    freq = lax.fori_loop(
+        0, retained, lambda j, held: jnp.where(row // 2 == j, freq_ref[j], held), jnp.zeros(shape, jnp.int32)
+    )
+    turn = 2.0 * math.pi / NFFT
+    angle = turn * (freq * step % NFFT).astype(F32)
+    window = 0.5 - 0.5 * jnp.cos(turn * iota((1, NFFT), 1).astype(F32))
     weighting = window / jnp.sqrt(jnp.sum(window * window))
-    table = jnp.stack([jnp.cos(angle), -jnp.sin(angle)], axis=1) * weighting[None, None, :]
-    return table.reshape(-1, window_len).astype(BF16)
+    return (jnp.where(row % 2 == 0, jnp.cos(angle), -jnp.sin(angle)) * weighting).astype(BF16)
 
 
 def iota(shape, dim):
@@ -40,9 +42,9 @@
 
 
 def kernel(
-    cfg, start_ref, basis_ref, series_ref, modes_ref, spec_ref,
-    hist, coef, moved, shifted, gram, packed, parts, total,
-    own_sem, z_send, z_recv, x_send, x_recv, s_send, s_recv, g_send, g_recv,
+    cfg, start_ref, freq_ref, series_ref, modes_ref, spec_ref,
+    taken, stage, hist, coef, moved, shifted, gram, packed, parts, total,
+    load_sem, z_send, z_recv, x_send, x_recv, s_send, s_recv, g_send, g_recv,
 ):
     npts, nsub, nfreq, snaps, planes, width, cols, blocks, groups, share = cfg
     n = npts * nsub
@@ -75,25 +77,51 @@
 
     pl.semaphore_wait(barrier, n - 1 + nfreq - 1)
 
+    own_rows = pl.ds(pl.multiple_of(me * snaps, snaps), snaps)
+
     def z_copy(c, i):
-        other, where = z_device(i)
-        at = pl.multiple_of(other * width + lax.rem(c, pieces) * cols, cols)
         return pltpu.make_async_remote_copy(
-            src_ref=series_ref.at[c // pieces, :, pl.ds(at, cols)],
-            dst_ref=hist.at[c, pl.ds(pl.multiple_of(me * snaps, snaps), snaps)],
+            src_ref=stage.at[lax.rem(c // planes, 2), i - 1, lax.rem(c, planes)],
+            dst_ref=hist.at[c, own_rows],
             send_sem=z_send.at[c, i],
             recv_sem=z_recv.at[c, i],
-            device_id=where,
+            device_id=z_device(i)[1],
             device_id_type=MESH,
         )
 
-    def own_copy(c):
-        at = pl.multiple_of(me * width + lax.rem(c, pieces) * cols, cols)
-        return pltpu.make_async_copy(
-            series_ref.at[c // pieces, :, pl.ds(at, cols)],
-            hist.at[c, pl.ds(pl.multiple_of(me * snaps, snaps), snaps)],
-            own_sem.at[c],
-        )
+    def load(q, k):
+        at = pl.multiple_of(lax.rem(me + k + 1, n) * width + q * cols, cols)
+        slot = lax.rem(k, 2)
+        return pltpu.make_async_copy(series_ref.at[:, :, pl.ds(at, cols)], taken.at[slot], load_sem.at[slot])
+
+    def regroup(q, send):
+        load(q, 0).start()
+
+        @pl.loop(0, n)
+        def _(k):
+            @pl.when(k + 1 < n)
+            def _():
+                load(q, k + 1).start()
+
+            load(q, k).wait()
+            tile = jnp.swapaxes(taken[lax.rem(k, 2)], 0, 1)
+
+            @pl.when(k + 1 < n)
+            def _():
+                stage[lax.rem(q, 2), k] = tile
+                if send:
+                    z_copy(q * planes, k + 1).start()
+
+            @pl.when(k + 1 == n)
+            def _():
+                hist[pl.ds(q * planes, planes), own_rows, :] = tile
+
+    def z_sent(q):
+        @pl.loop(0, planes)
+        def _(p):
+            @pl.loop(1, n)
+            def _(i):
+                z_copy(q * planes + p, i).wait_send()
 
     def x_copy(c, i):
         other, where = x_device(i)
@@ -111,17 +139,17 @@
         def _(i):
             z_copy(c, i).start()
 
-        own_copy(c).start()
-
-    ahead = min(AHEAD, chunks)
-    for c in range(ahead):
+    regroup(0, True)
+    ahead = planes - 1
+    for c in range(1, ahead):
         z_start(c)
 
     firsts = [min(max(SPACING * b - JITTER, 0), length - SPAN) for b in range(blocks)]
     gap = iota((NFFT, SPAN), 1) - iota((NFFT, SPAN), 0)
+    basis = dft_basis(freq_ref, groups * PACK)
     for b in range(blocks):
         move = jnp.where(gap == start_ref[b] - firsts[b], 1.0, 0.0).astype(BF16)
-        shifted[b] = jnp.dot(basis_ref[...], move, preferred_element_type=F32).astype(BF16)
+        shifted[b] = jnp.dot(basis, move, preferred_element_type=F32).astype(BF16)
     gram[...] = jnp.zeros_like(gram)
 
     def add_gram(g, tile):
@@ -140,7 +168,15 @@
         def _():
             z_start(c + ahead)
 
-        own_copy(c).wait()
+        @pl.when((lax.rem(c, planes) == 0) & (c + planes < chunks))
+        def _():
+            q = c // planes + 1
+
+            @pl.when(q > 1)
+            def _():
+                z_sent(q - 2)
+
+            regroup(q, False)
 
         @pl.loop(1, n)
         def _(i):
@@ -244,6 +280,7 @@
         return jnp.sum(jnp.where(eye, vec, 0.0), axis=0, keepdims=True)
 
     mixes, gains = [], []
+    spec = jnp.zeros((1, lanes), F32)
     for g in range(local):
         choose = chooser(g)
         block = lax.dot_general(
@@ -254,7 +291,9 @@
         for _ in range(ITERS):
             out = over(both, vec)
             vec = flat(out) / jnp.sqrt(down(same, out * out))
-        spec_ref[g : g + 1, :] = down(same, over(both, vec) * upright(vec))
+        values = down(same, over(both, vec) * upright(vec))
+        slot = (slot_r % 2 == 0) & (slot_r < 2 * PACK) & (slot_l == g * PACK + slot_r // 2)
+        spec += down(jnp.where(slot, 1.0, 0.0), upright(values))
         low_bf = vec.astype(BF16)
         low = low_bf.astype(F32)
         low_up = upright(low)
@@ -265,10 +304,12 @@
         mixes.append(mix.astype(BF16))
         gains.append(jnp.sum(jnp.where(mode_first, gain, 0.0), axis=1, keepdims=True))
 
+    spec_ref[...] = spec
+
     @pl.loop(0, planes)
     def _(p):
         for q in range(pieces):
-            c = p * pieces + q
+            c = q * planes + p
             at = pl.ds(q * cols, cols)
             for g in range(local):
                 modes_ref[mine * planes + p, pl.ds(g * 2 * PACK, 2 * PACK), at] = (
@@ -283,13 +324,12 @@
 
     @pl.loop(0, chunks)
     def _(c):
-        @pl.loop(1, n)
-        def _(i):
-            z_copy(c, i).wait_send()
-
         @pl.loop(1, nfreq)
         def _(i):
             x_copy(c, i).wait_send()
+
+    for q in range(max(0, pieces - 2), pieces):
+        z_sent(q)
 
 
 def shards(series, block_start, freq_index):
@@ -306,23 +346,23 @@
     chunks = planes * (width // cols)
     share = -(-rows // (8 * n)) * 8
     lanes = max(128, local * 32)
-    basis = dft_basis(freq_index, NFFT)
-    turned = jnp.transpose(series, (1, 0, 2))
     cfg = (npts, nsub, nfreq, snaps, planes, width, cols, blocks, groups, share)
     dma = pltpu.SemaphoreType.DMA
     raw, spec = pl.pallas_call(
         functools.partial(kernel, cfg),
         out_shape=(
             jax.ShapeDtypeStruct((nfreq * planes, local * 2 * PACK, width), F32),
-            jax.ShapeDtypeStruct((local, rows), F32),
+            jax.ShapeDtypeStruct((1, lanes), F32),
         ),
         in_specs=[
             pl.BlockSpec(memory_space=pltpu.SMEM),
-            pl.BlockSpec(memory_space=pltpu.VMEM),
+            pl.BlockSpec(memory_space=pltpu.SMEM),
             pl.BlockSpec(memory_space=pl.ANY),
         ],
         out_specs=(pl.BlockSpec(memory_space=pltpu.VMEM), pl.BlockSpec(memory_space=pltpu.VMEM)),
         scratch_shapes=[
+            pltpu.VMEM((2, snaps, planes, cols), BF16),
+            pltpu.VMEM((min(2, width // cols), n - 1, planes, snaps, cols), BF16),
             pltpu.VMEM((chunks, n * snaps, cols), BF16),
             pltpu.VMEM((chunks, groups, rows, cols), BF16),
             pltpu.VMEM((nfreq - 1, chunks, local, rows, cols), BF16),
@@ -331,7 +371,7 @@
             pltpu.VMEM((n * share, lanes), F32),
             pltpu.VMEM((n, share, lanes), F32),
             pltpu.VMEM((n * share, lanes), F32),
-            dma((chunks,)),
+            dma((2,)),
             dma((chunks, n)),
             dma((chunks, n)),
             dma((chunks, nfreq)),
@@ -344,10 +384,10 @@
         compiler_params=pltpu.CompilerParams(
             collective_id=0, has_side_effects=True, vmem_limit_bytes=60 * 1024 * 1024
         ),
-    )(block_start, basis, turned)
+    )(block_start, freq_index, series)
     modes = raw.reshape(nfreq * planes, local, 2, PACK, width).transpose(2, 1, 3, 0, 4)
     modes = modes.reshape(2, local * PACK, nfreq * planes, width)
-    return modes, spec[:, : 2 * PACK : 2].reshape(local * PACK)
+    return modes, spec[0, : local * PACK]
 
 
 def solution(mesh):

time: 432 us -> 410 us (0.949)
  local copies, waits for them, and re-layouts: 24.2 us -> 4.69 us
    unnamed x1 -> x2, local copies, waits for them, and re-layouts: 18.5 us -> 0.01 us
where the time goes in v2:
time: 410 us
  Pallas kernels  404 us (99%)
  local copies, waits for them, and re-layouts  4.69 us (1%)
    pallas_call x1, Pallas kernels, shards(): pl.pallas_call(functools.partial(kernel, cfg), out_shape=(jax.ShapeDtypeS...  404 us

profile of v2, /device:TPU:0, one launch (start us, length us, event | category | flops | bytes accessed | tf_op | source)
XLA Modules:
  0.0 409.8 jit_solution(13478270075978258166)
XLA Ops:
  0.6 404.5 %shard_map.50 = (f32[8,64,1024]{2,1,0:T(8,128)}, f32[1,128]{1,0:T(1,128)}) custom-call(s32[15]{0:T(128)} %start_ref.1, s32[64]{0:T(128)} %freq_ref.1, bf16[256,4,8192]{2,1,0:T(4,128)(2,1)} %series_ref.1), custom_call_target="tpu_custom_call" | custom-call | tf_op jit(solution)/shard_map/pallas_call | solution.py:351
  405.1 0.0 copy-start
  405.1 4.2 %copy.5 = f32[2,4,8,8,1024]{4,3,2,1,0:T(8,128)} copy(f32[2,4,8,8,1024]{4,2,0,1,3:T(8,128)} %bitcast.7) | data formatting | bytes 4194304 | tf_op jit(solution)/shard_map/transpose | solution.py:388
  409.3 0.0 copy-done
  409.3 0.5 slice_bitcast_fusion
Async XLA Ops:
  405.1 4.2 %copy-start = (f32[1,128]{1,0:T(1,128)S(1)}, f32[1,128]{1,0:T(1,128)}, u32[]{:S(2)}) copy-start(f32[1,128]{1,0:T(1,128)} %get-tuple-element.5) | copy-start | bytes 1540

commit v3 on v2

--- a/solution.py
+++ b/solution.py
@@ -43,12 +43,13 @@
 
 def kernel(
     cfg, start_ref, freq_ref, series_ref, modes_ref, spec_ref,
-    taken, stage, hist, coef, moved, shifted, gram, packed, parts, total,
+    taken, stage, hist, coef, moved, shifted, gram, packed, parts, total, turning,
     load_sem, z_send, z_recv, x_send, x_recv, s_send, s_recv, g_send, g_recv,
 ):
-    npts, nsub, nfreq, snaps, planes, width, cols, blocks, groups, share = cfg
+    npts, nsub, nfreq, snaps, planes, width, part, cols, blocks, groups, share = cfg
     n = npts * nsub
-    pieces = width // cols
+    pieces = width // part
+    fold = cols // part
     chunks = planes * pieces
     local = groups // nfreq
     rows = blocks * 2 * PACK
@@ -90,9 +91,9 @@
         )
 
     def load(q, k):
-        at = pl.multiple_of(lax.rem(me + k + 1, n) * width + q * cols, cols)
+        at = pl.multiple_of(lax.rem(me + k + 1, n) * width + q * part, part)
         slot = lax.rem(k, 2)
-        return pltpu.make_async_copy(series_ref.at[:, :, pl.ds(at, cols)], taken.at[slot], load_sem.at[slot])
+        return pltpu.make_async_copy(series_ref.at[:, :, pl.ds(at, part)], taken.at[slot], load_sem.at[slot])
 
     def regroup(q, send):
         load(q, 0).start()
@@ -123,11 +124,17 @@
             def _(i):
                 z_copy(q * planes + p, i).wait_send()
 
+    def spot(c):
+        q = c // planes
+        at = pl.multiple_of(lax.rem(q, fold) * part, part)
+        return q // fold * planes + lax.rem(c, planes), pl.ds(at, part)
+
     def x_copy(c, i):
         other, where = x_device(i)
+        wide, at = spot(c)
         return pltpu.make_async_remote_copy(
-            src_ref=coef.at[c, pl.ds(other * local, local)],
-            dst_ref=moved.at[i - 1, c],
+            src_ref=coef.at[wide, pl.ds(other * local, local), :, at],
+            dst_ref=moved.at[i - 1, wide, :, :, at],
             send_sem=x_send.at[c, i],
             recv_sem=x_recv.at[c, i],
             device_id=where,
@@ -156,11 +163,13 @@
         gram[g] += lax.dot_general(tile, tile, (((1,), (1,)), ((), ())), preferred_element_type=F32)
 
     def take_moved(c):
+        wide, at = spot(c)
+
         @pl.loop(1, nfreq)
         def _(i):
             x_copy(c, i).wait_recv()
             for g in range(local):
-                add_gram(g, moved[i - 1, c, g])
+                add_gram(g, moved[i - 1, wide, g, :, at])
 
     @pl.loop(0, chunks)
     def _(c):
@@ -182,16 +191,17 @@
         def _(i):
             z_copy(c, i).wait_recv()
 
+        wide, at = spot(c)
         for b in range(blocks):
             out = jnp.dot(shifted[b], hist[c, firsts[b] : firsts[b] + SPAN, :], preferred_element_type=F32)
-            coef[c, :, b * 2 * PACK : (b + 1) * 2 * PACK, :] = out.astype(BF16).reshape(groups, 2 * PACK, cols)
+            coef[wide, :, b * 2 * PACK : (b + 1) * 2 * PACK, at] = out.astype(BF16).reshape(groups, 2 * PACK, part)
 
         @pl.loop(1, nfreq)
         def _(i):
             x_copy(c, i).start()
 
         for g in range(local):
-            add_gram(g, coef[c, mine * local + g])
+            add_gram(g, coef[wide, mine * local + g, :, at])
 
         @pl.when(c > 0)
         def _():
@@ -279,48 +289,55 @@
     def flat(vec):
         return jnp.sum(jnp.where(eye, vec, 0.0), axis=0, keepdims=True)
 
-    mixes, gains = [], []
+    every = range(local)
+    chosen = [chooser(g) for g in every]
+    summed = total[:rows, :]
+    compact = [
+        lax.dot_general(summed, chosen[g], (((1,), (1,)), ((), ())), precision=HIGHEST, preferred_element_type=F32)
+        * same
+        for g in every
+    ]
+    half = [exact_dot(turn, compact[g]) for g in every]
+    cross = [(compact[g] - exact_dot(half[g], turn)) * scale for g in every]
+    vecs = [head for g in every]
+    for _ in range(ITERS):
+        outs = [over(cross[g], vecs[g]) for g in every]
+        sizes = [down(same, outs[g] * outs[g]) for g in every]
+        vecs = [flat(outs[g]) / jnp.sqrt(sizes[g]) for g in every]
+    lows = [vecs[g].astype(BF16).astype(F32) for g in every]
+    ups = [upright(lows[g]) for g in every]
+    energy = [down(same, over(cross[g], lows[g]) * ups[g]) * blocks for g in every]
+    turned = [flat(over(turn, lows[g])) for g in every]
+    gains = [
+        jnp.sum(jnp.where(mode_first, lax.rsqrt(energy[g] + 1e-06), 0.0), axis=1, keepdims=True) for g in every
+    ]
+    mixes = [
+        jnp.where(mode_same, jnp.where(mode_r < PACK, lows[g], turned[g]), 0.0).astype(BF16) for g in every
+    ]
+    values = [down(same, over(cross[g], vecs[g]) * upright(vecs[g])) for g in every]
     spec = jnp.zeros((1, lanes), F32)
-    for g in range(local):
-        choose = chooser(g)
-        block = lax.dot_general(
-            total[:rows, :], choose, (((1,), (1,)), ((), ())), precision=HIGHEST, preferred_element_type=F32
-        ) * same
-        both = (block - exact_dot(exact_dot(turn, block), turn)) * scale
-        vec = head
-        for _ in range(ITERS):
-            out = over(both, vec)
-            vec = flat(out) / jnp.sqrt(down(same, out * out))
-        values = down(same, over(both, vec) * upright(vec))
+    for g in every:
         slot = (slot_r % 2 == 0) & (slot_r < 2 * PACK) & (slot_l == g * PACK + slot_r // 2)
-        spec += down(jnp.where(slot, 1.0, 0.0), upright(values))
-        low_bf = vec.astype(BF16)
-        low = low_bf.astype(F32)
-        low_up = upright(low)
-        energy = down(same, over(both, low) * low_up) * (points * blocks / points)
-        gain = lax.rsqrt(energy + 1e-06)
-        turned = flat(over(turn, low))
-        mix = jnp.where(mode_same, jnp.where(mode_r < PACK, low, turned), 0.0)
-        mixes.append(mix.astype(BF16))
-        gains.append(jnp.sum(jnp.where(mode_first, gain, 0.0), axis=1, keepdims=True))
-
+        spec += down(jnp.where(slot, 1.0, 0.0), upright(values[g]))
     spec_ref[...] = spec
 
-    @pl.loop(0, planes)
-    def _(p):
-        for q in range(pieces):
-            c = q * planes + p
-            at = pl.ds(q * cols, cols)
-            for g in range(local):
-                modes_ref[mine * planes + p, pl.ds(g * 2 * PACK, 2 * PACK), at] = (
-                    jnp.dot(mixes[g], coef[c, mine * local + g], preferred_element_type=F32) * gains[g]
+    @pl.loop(0, width // cols)
+    def _(q):
+        at = pl.ds(pl.multiple_of(q * cols, cols), cols)
+        for g in every:
+            for p in range(planes):
+                turning[g, mine * planes + p] = (
+                    jnp.dot(mixes[g], coef[q * planes + p, mine * local + g], preferred_element_type=F32) * gains[g]
                 )
-            for i in range(1, nfreq):
-                source = lax.rem(mine + nfreq - i, nfreq)
-                for g in range(local):
-                    modes_ref[source * planes + p, pl.ds(g * 2 * PACK, 2 * PACK), at] = (
-                        jnp.dot(mixes[g], moved[i - 1, c, g], preferred_element_type=F32) * gains[g]
+                for i in range(1, nfreq):
+                    source = lax.rem(mine + nfreq - i, nfreq)
+                    turning[g, source * planes + p] = (
+                        jnp.dot(mixes[g], moved[i - 1, q * planes + p, g], preferred_element_type=F32) * gains[g]
                     )
+        for g in every:
+            tile = jnp.swapaxes(turning[g], 0, 1)
+            modes_ref[0, g * PACK : (g + 1) * PACK, :, at] = tile[:PACK]
+            modes_ref[1, g * PACK : (g + 1) * PACK, :, at] = tile[PACK:]
 
     @pl.loop(0, chunks)
     def _(c):
@@ -338,20 +355,22 @@
     n = npts * nsub
     width = plane // n
     cols = min(256, width)
+    part = min(128, width)
     blocks = block_start.shape[0]
     retained = freq_index.shape[0]
     groups = retained // PACK
     local = groups // nfreq
     rows = blocks * 2 * PACK
-    chunks = planes * (width // cols)
+    chunks = planes * (width // part)
+    wides = planes * (width // cols)
     share = -(-rows // (8 * n)) * 8
     lanes = max(128, local * 32)
-    cfg = (npts, nsub, nfreq, snaps, planes, width, cols, blocks, groups, share)
+    cfg = (npts, nsub, nfreq, snaps, planes, width, part, cols, blocks, groups, share)
     dma = pltpu.SemaphoreType.DMA
-    raw, spec = pl.pallas_call(
+    modes, spec = pl.pallas_call(
         functools.partial(kernel, cfg),
         out_shape=(
-            jax.ShapeDtypeStruct((nfreq * planes, local * 2 * PACK, width), F32),
+            jax.ShapeDtypeStruct((2, local * PACK, nfreq * planes, width), F32),
             jax.ShapeDtypeStruct((1, lanes), F32),
         ),
         in_specs=[
@@ -361,16 +380,17 @@
         ],
         out_specs=(pl.BlockSpec(memory_space=pltpu.VMEM), pl.BlockSpec(memory_space=pltpu.VMEM)),
         scratch_shapes=[
-            pltpu.VMEM((2, snaps, planes, cols), BF16),
-            pltpu.VMEM((min(2, width // cols), n - 1, planes, snaps, cols), BF16),
-            pltpu.VMEM((chunks, n * snaps, cols), BF16),
-            pltpu.VMEM((chunks, groups, rows, cols), BF16),
-            pltpu.VMEM((nfreq - 1, chunks, local, rows, cols), BF16),
+            pltpu.VMEM((2, snaps, planes, part), BF16),
+            pltpu.VMEM((min(2, width // part), n - 1, planes, snaps, part), BF16),
+            pltpu.VMEM((chunks, n * snaps, part), BF16),
+            pltpu.VMEM((wides, groups, rows, cols), BF16),
+            pltpu.VMEM((nfreq - 1, wides, local, rows, cols), BF16),
             pltpu.VMEM((blocks, 2 * retained, SPAN), BF16),
             pltpu.VMEM((local, rows, rows), F32),
             pltpu.VMEM((n * share, lanes), F32),
             pltpu.VMEM((n, share, lanes), F32),
             pltpu.VMEM((n * share, lanes), F32),
+            pltpu.VMEM((local, nfreq * planes, 2 * PACK, cols), F32),
             dma((2,)),
             dma((chunks, n)),
             dma((chunks, n)),
@@ -385,8 +405,6 @@
             collective_id=0, has_side_effects=True, vmem_limit_bytes=60 * 1024 * 1024
         ),
     )(block_start, freq_index, series)
-    modes = raw.reshape(nfreq * planes, local, 2, PACK, width).transpose(2, 1, 3, 0, 4)
-    modes = modes.reshape(2, local * PACK, nfreq * planes, width)
     return modes, spec[0, : local * PACK]
 
 

time: 410 us -> 409 us (level)
    transpose x1 -> x0, local copies, waits for them, and re-layouts: 4.17 us -> none  [shards(): raw.reshape(nfreq * planes, local, 2, PACK, width).transpose(2, 1, 3, 0, 4)]
where the time goes in v3:
time: 409 us; the launch traced here: 408 us
  Pallas kernels  403 us (99%)
  local copies, waits for them, and re-layouts  4.3 us (1%)
    pallas_call x1, Pallas kernels, shards(): pl.pallas_call(functools.partial(kernel, cfg), out_shape=(jax.ShapeDtypeS...  403 us

profile of v3, /device:TPU:0, one launch (start us, length us, event | category | flops | bytes accessed | tf_op | source)
XLA Modules:
  0.0 407.9 jit_solution(13070295529781659626)
XLA Ops:
  0.6 403.0 %shard_map.50 = (f32[2,32,8,1024]{3,2,1,0:T(8,128)}, f32[1,128]{1,0:T(1,128)}) custom-call(s32[15]{0:T(128)} %start_ref.1, s32[64]{0:T(128)} %freq_ref.1, bf16[256,4,8192]{2,1,0:T(4,128)(2,1)} %series_ref.1), custom_call_target="tpu_custom_call" | custom-call | tf_op jit(solution)/shard_map/pallas_call | solution.py:370
  403.6 1.1 slice_bitcast_fusion
  404.7 3.2 copy.6
